TPU v7x, 32 devices: a whole 2x2x4 slice. The times are simulated.
32 devices in a mesh: dp: 8 (over z, y), section: 4 (over x, core).
Axes of the slice: x: 2, y: 2, z: 4, core: 2. Of those that a mesh axis runs over, the one named last changes fastest.
Arguments:
- tokens: bfloat16 [8192, 1024], P('dp'), may hold values from -6 to 6
- doc_lengths: int32 [16, 4], P('dp'), may hold values from 1 to 256, 512 in all within a row
- first_weights: bfloat16 [4, 1024, 4096], P('section'), may hold values from -0.1875 to 0.1875
- down_weights: bfloat16 [4, 2048, 1024], P('section'), may hold values from -0.09375 to 0.09375
- norm_gains: float32 [4, 2, 1024], P('section'), may hold values from 0.5 to 1.5
- norm_biases: float32 [4, 2, 1024], P('section'), may hold values from -1.2 to 1.2
- cotangent: bfloat16 [8192, 1024], P('dp'), may hold values from -6 to 6
Outputs:
- section_outputs: bfloat16 [4, 8192, 1024], P('section', 'dp')
- input_grads: bfloat16 [4, 8192, 1024], P('section', 'dp')
- first_grad: float32 [4, 1024, 4096], P('section', 'dp')
- down_grad: float32 [4, 2048, 1024], P('section', 'dp')
- gain_grad: float32 [4, 2, 1024], P('section', None, 'dp')
- bias_grad: float32 [4, 2, 1024], P('section', None, 'dp')
Inputs may be any that keep to these rules, and one draw needn't show every extreme that they name: `doc_lengths`: each row's lengths add up to 512.
All inputs are finite; a program needn't handle non-finite values.
Results may differ from a plain program's by a relative error of at most 0.02.
Values may be sent and summed in bfloat16 or wider, within the bound.
A program may use at most 384 MiB of HBM per device.

v0:
```python
import functools

import jax
import jax.numpy as jnp
from jax import lax
from jax.experimental import pallas as pl
from jax.experimental.pallas import tpu as pltpu
from jax.sharding import PartitionSpec as P

HEADS = 16
HEAD = 64
PAIRS = HEADS // 2
LANES = 2 * HEAD
eps = 1e-05
masked_value = -1e30
score_scale = HEAD ** (-0.5)
MESH = pl.DeviceIdType.MESH
low = jnp.bfloat16
f32 = jnp.float32
tanh_linear = (2.0 / 3.141592653589793) ** 0.5
tanh_cubic = tanh_linear * 0.044715


def ring_place(index, count):
    return jnp.where(index % 2 == 0, index // 2, count - 1 - index // 2)


def ring_index(place, count):
    return jnp.where(place < count // 2, 2 * place, 2 * (count - 1 - place) + 1)


def dot(left, right):
    return jnp.dot(left, right, preferred_element_type=f32)


def dot_cols(left, right):
    return lax.dot_general(left, right, (((1,), (1,)), ((), ())), preferred_element_type=f32)


def whiten(values):
    average = jnp.mean(values, axis=-1, keepdims=True)
    centered = values - average
    variance = jnp.mean(centered * centered, axis=-1, keepdims=True)
    spread = lax.rsqrt(variance + eps)
    return centered * spread, spread


def whiten_back(grad, normal, spread):
    first = jnp.mean(grad, axis=-1, keepdims=True)
    second = jnp.mean(grad * normal, axis=-1, keepdims=True)
    return spread * (grad - first - normal * second)


def gelu_both(u):
    square = u * u
    half = 0.5 + 0.5 * jnp.tanh(u * (tanh_linear + tanh_cubic * square))
    value = u * half
    slope = half + value * (1.0 - half) * (2.0 * tanh_linear + 6.0 * tanh_cubic * square)
    return value, slope


def layers_kernel(
    count,
    tokens,
    cotangent,
    lengths,
    first,
    down,
    gains,
    biases,
    outputs,
    input_grads,
    first_grad,
    down_grad,
    small_out,
    pool,
    sends,
    stash,
    spreads,
    kept,
    mask,
    total,
    lhs,
    hidden_t,
    rhs,
    dz_down,
    affine,
    log_t,
    log_rows,
    delta_t,
    sums,
    small,
    small_pair,
    small_sum,
    small_recv,
    weight_ls,
    weight_ss,
    weight_rs,
    row_ls,
    hop_ss,
    hop_rs,
    out_ls,
    out_ss,
    out_rs,
    ready,
    pair_ready,
    first_ss,
    first_rs,
    pair_ss,
    pair_rs,
    ring_ss,
    ring_rs,
    small_sems,
    small_ss,
    small_rs,
    grad_ls,
):
    rows, width = pool.shape[1:]
    row_len = rhs.shape[1]
    unit = row_len // 2
    blocks = unit // rows
    dp = lax.axis_index("dp")
    section = lax.axis_index("section")
    section_count = lax.axis_size("section")
    core = lax.rem(section, 2)
    peer = section + 1 - 2 * core
    early = section < 2
    late = section >= 2
    partner = lax.rem(section + 2, section_count)
    place = ring_place(dp, count)
    left = ring_index(lax.rem(place + count - 1, count), count)
    right = ring_index(lax.rem(place + 1, count), count)

    barrier = pltpu.get_barrier_semaphore()

    def greet(step, carry):
        other = lax.rem(dp + step, count)
        pl.semaphore_signal(barrier, inc=1, device_id=(other, section), device_id_type=MESH)
        return carry

    lax.fori_loop(1, count, greet, 0)
    for other in (peer, partner):
        pl.semaphore_signal(barrier, inc=1, device_id=(dp, other), device_id_type=MESH)

    def own_chunk(k):
        if k < 4:
            return first.at[:, :, pl.ds(k * width, width)], 4 * core + k
        return down.at[pl.ds((k - 4) * count, count)], 8 + 2 * core + k - 4

    def weight_local(k):
        source, chunk = own_chunk(k)
        target = pool.at[pl.ds(chunk * count, count)]
        return pltpu.make_async_copy(source, target, weight_ls.at[k])

    def to_peer(source, target, send_sem, recv_sem):
        return pltpu.make_async_remote_copy(
            src_ref=source,
            dst_ref=target,
            send_sem=send_sem,
            recv_sem=recv_sem,
            device_id=(dp, peer),
            device_id_type=MESH,
        )

    def weight_remote(k):
        source, chunk = own_chunk(k)
        target = pool.at[pl.ds(chunk * count, count)]
        return to_peer(source, target, weight_ss.at[k], weight_rs.at[k])

    def affine_local(i):
        source = (gains, biases)[i].at[0]
        return pltpu.make_async_copy(source, affine.at[core, i], weight_ls.at[6 + i])

    def affine_remote(i):
        source = (gains, biases)[i].at[0]
        return to_peer(source, affine.at[core, i], weight_ss.at[6 + i], weight_rs.at[6 + i])

    def await_chunk(chunk):
        owner = 1 if 4 <= chunk < 8 or chunk >= 10 else 0
        k = chunk % 4 if chunk < 8 else 4 + chunk % 2

        @pl.when(core == owner)
        def _():
            weight_local(k).wait()

        @pl.when(core != owner)
        def _():
            weight_remote(k).wait_recv()

    def await_feed(i):
        @pl.when(core == 0)
        def _():
            weight_remote(i).wait_recv()

        @pl.when(core == 1)
        def _():
            weight_local((i + 2) % 4).wait()

        if i < 2:
            weight_local(4 + i).wait()
        else:
            weight_remote(2 + i).wait_recv()

    def weight(chunk):
        return pool[pl.ds(chunk * count, count)].reshape(width, width)

    def weight_cols(chunk, some):
        return pool[pl.ds(chunk * count, count), :, some].reshape(width, width // 2)

    def weight_rows(chunk, half):
        start = chunk * count + half * (count // 2)
        return pool[pl.ds(start, count // 2)].reshape(width // 2, width)

    def stash_at(place_in):
        return stash.at[pl.ds(place_in * blocks, blocks)]

    def stash_read(place_in):
        return stash[pl.ds(place_in * blocks, blocks)].reshape(unit, width)

    def stash_write(place_in, value):
        stash[pl.ds(place_in * blocks, blocks)] = value.astype(low).reshape(blocks, rows, width)

    def row_copy(u, source, target, sem):
        start = (core * 2 + u) * blocks
        return pltpu.make_async_copy(source.at[pl.ds(start, blocks)], target, sem)

    def token_copy(u):
        return row_copy(u, tokens, stash_at(u), row_ls.at[u])

    def cotangent_copy(u):
        return row_copy(u, cotangent, sends.at[pl.ds((6 + u) * blocks, blocks)], row_ls.at[2 + u])

    def hop_copy(k, part):
        u = k % 2
        some = pl.ds(part * (blocks // 2), blocks // 2)
        arriving = pl.ds(u * blocks + part * (blocks // 2), blocks // 2)
        grad_arriving = pl.ds((6 + u) * blocks + part * (blocks // 2), blocks // 2)
        return pltpu.make_async_remote_copy(
            src_ref=kept.at[1, u, some],
            dst_ref=stash.at[arriving] if k < 2 else sends.at[grad_arriving],
            send_sem=hop_ss.at[k, part],
            recv_sem=hop_rs.at[k, part],
            device_id=(dp, partner),
            device_id_type=MESH,
        )

    def out_copies(kind, u):
        target = (outputs, input_grads)[kind]
        place_out = target.at[pl.ds((core * 2 + u) * blocks, blocks)]
        k = 2 * kind + u
        own, other = (core, 1 - core) if kind == 0 else (1 - core, core)
        return (
            pltpu.make_async_copy(kept.at[own, u], place_out, out_ls.at[k]),
            to_peer(kept.at[other, u], place_out, out_ss.at[k], out_rs.at[k]),
        )

    def outputs_sent(u):
        local_copy, remote_copy = out_copies(0, u)
        local_copy.wait()
        remote_copy.wait_send()

        @pl.when(early)
        def _():
            for part in range(2):
                hop_copy(u, part).wait_send()

    for k in range(6):
        weight_local(k).start()
    for i in range(2):
        affine_local(i).start()

    @pl.when(early)
    def _():
        for u in range(2):
            token_copy(u).start()

    @pl.when(late)
    def _():
        for u in range(2):
            cotangent_copy(u).start()

    pl.semaphore_wait(barrier, count + 1)
    for i in range(2):
        affine_remote(i).start()
    for k in range(6):
        weight_remote(k).start()

    sums[...] = jnp.zeros_like(sums)
    log_rows[...] = jnp.zeros_like(log_rows)
    small[...] = jnp.zeros_like(small)
    for i in range(2):
        affine_local(i).wait()
        affine_remote(i).wait_recv()

    def gain(sub, which):
        return affine[sub, 0, which : which + 1, :]

    def bias(sub, which):
        return affine[sub, 1, which : which + 1, :]

    ends = [lengths[core, 0]]
    for j in range(1, lengths.shape[1]):
        ends.append(ends[-1] + lengths[core, j])

    def mask_of(shape, query_axis, first_query, first_key):
        query = lax.broadcasted_iota(jnp.int32, shape, query_axis) + first_query
        key = lax.broadcasted_iota(jnp.int32, shape, 1 - query_axis) + first_key
        apart = jnp.zeros(shape, jnp.int32)
        for end in ends:
            apart += (query >= end).astype(jnp.int32) - (key >= end).astype(jnp.int32)
        return jnp.where((apart == 0) & (key <= query), 0.0, masked_value)

    def projected(part, lanes, u=0, halves=1):
        span = pl.ds((2 * part + u) * blocks, halves * blocks)
        return sends[span, :, lanes].reshape(halves * unit, LANES)

    def half_lanes(h, scale):
        lane = lax.broadcasted_iota(jnp.int32, (1, LANES), 1)
        return jnp.where((lane >= h * HEAD) & (lane < (h + 1) * HEAD), scale, 0.0)

    def pair_lanes(p):
        return pl.ds(pl.multiple_of(p * LANES, LANES), LANES)

    def branch():
        return total[pl.ds(2 * blocks, blocks)].reshape(unit, width)

    def add_branch(term, begin):
        value = term if begin else branch() + term
        total[pl.ds(2 * blocks, blocks)] = value.reshape(blocks, rows, width)

    size = min(rows, 64)
    groups = rows // size

    def by_rows(body, part=None):
        def step(i, carry):
            block, start = i // groups, pl.multiple_of(lax.rem(i, groups) * size, size)
            body(block, pl.ds(start, size), pl.ds(pl.multiple_of(i * size, size), size))
            return carry

        half = unit // size // 2
        begin, end = (0, 2 * half) if part is None else (part * half, (part + 1) * half)
        lax.fori_loop(begin, end, step, 0, unroll=True)

    def add_sums(sub, which, grad, normal):
        row = 4 * sub + which
        sums[row] += jnp.sum((grad * normal).reshape(size // 8, 8, width), axis=0)
        sums[row + 2] += jnp.sum(grad.reshape(size // 8, 8, width), axis=0)

    def normed_input(sub, values):
        return (whiten(values)[0] * gain(sub, 0) + bias(sub, 0)).astype(low)

    def await_input(u, half):
        @pl.when(late)
        def _():
            hop_copy(u, half).wait_recv()

        if half == 0:

            @pl.when(early)
            def _():
                token_copy(u).wait()

    def await_grad(u, half):
        @pl.when(early)
        def _():
            hop_copy(2 + u, half).wait_recv()

        if half == 0:

            @pl.when(late)
            def _():
                cotangent_copy(u).wait()

    def send_part(stage, k, part):
        @pl.when(stage)
        def _():
            hop_copy(k, part).start()

    def attention_forward(u):
        span = slice(u * unit, (u + 1) * unit)

        def norm_in(block, some, _):
            values = stash[u * blocks + block, some, :].astype(f32)
            stash[4 * blocks + block, some, :] = normed_input(0, values)

        for half in range(2):
            await_input(u, half)
            by_rows(norm_in, half)
            if u == 0:
                part_blocks = blocks // 2
                normed = stash[pl.ds(4 * blocks + half * part_blocks, part_blocks)]
                for part in range(3):
                    if half == 0:
                        await_chunk(part)
                    value = dot(normed.reshape(unit // 2, width), weight(part)).astype(low)
                    target = pl.ds(2 * part * blocks + half * part_blocks, part_blocks)
                    sends[target] = value.reshape(part_blocks, rows, width)
        for part in range(3) if u == 1 else ():
            value = dot(stash_read(4), weight(part)).astype(low)
            sends[pl.ds((2 * part + u) * blocks, blocks)] = value.reshape(blocks, rows, width)
        lhs[0, :, span] = stash_read(4).T
        for i in range(u + 1):
            mask[i * unit : (i + 1) * unit, :] = mask_of((unit, unit), 0, u * unit, i * unit)
        lane = lax.broadcasted_iota(jnp.int32, (unit, LANES), 1)

        def pair(p, carry):
            lanes = pair_lanes(p)
            query = projected(0, lanes, u).astype(f32)
            key = projected(1, lanes, 0, u + 1)
            value = projected(2, lanes, 0, u + 1)
            added = jnp.concatenate([mask[i * unit : (i + 1) * unit, :] for i in range(u + 1)], 1)
            context = None
            for h in range(2):
                scores = dot_cols((query * half_lanes(h, score_scale)).astype(low), key)
                scores = scores + added
                top = jnp.max(scores, axis=-1, keepdims=True)
                exponent = jnp.exp(scores - top)
                summed = jnp.sum(exponent, axis=-1, keepdims=True)
                part = dot(exponent.astype(low), value) * (1.0 / summed)
                context = part if h == 0 else jnp.where(lane < HEAD, context, part)
                log_total = top + jnp.log(summed)
                log_rows[...] = jnp.where(lane == 2 * p + h, log_total, log_rows[...])
            rhs[3, span, lanes] = context.astype(low)
            return carry

        lax.fori_loop(0, PAIRS, pair, 0, unroll=2)
        log_t[u] = log_rows[...].T[:HEADS]
        if u == 0:
            await_chunk(3)
        add_branch(dot_cols(rhs[3, span, :], weight(3)), True)

        def norm_out(block, some, across):
            normal, spread = whiten(total[2 * blocks + block, some, :])
            stash[(2 + u) * blocks + block, some, :] = normal.astype(low)
            spreads[pl.ds(u * unit + across.start, size), 0:1] = spread
            middle = stash[u * blocks + block, some, :].astype(f32)
            middle = (middle + (normal * gain(0, 1) + bias(0, 1))).astype(low)
            kept[0, u, block, some, :] = middle
            stash[4 * blocks + block, some, :] = normed_input(1, middle.astype(f32))

        by_rows(norm_out)

    def feed_forward(u):
        span = slice(u * unit, (u + 1) * unit)
        lhs[2, :, span] = stash_read(4).T
        for i in range(4):
            c = lax.rem(2 * core + i, 4) if u == 0 else i
            if u == 0:
                await_feed(i)
            hidden, slope = gelu_both(dot(stash_read(4), weight(4 + c)))
            hidden = hidden.astype(low)
            rhs[4 + c, span, :] = slope.astype(low)
            hidden_t[pl.ds(pl.multiple_of(c * width, width), width), span] = hidden.T
            add_branch(dot(hidden, weight(8 + c)), i == 0)

        def norm_out(block, some, across):
            normal, spread = whiten(total[2 * blocks + block, some, :])
            stash[(5 + u) * blocks + block, some, :] = normal.astype(low)
            spreads[pl.ds(u * unit + across.start, size), 1:2] = spread
            middle = kept[0, u, block, some, :].astype(f32)
            output = middle + (normal * gain(1, 1) + bias(1, 1))
            kept[1, u, block, some, :] = output.astype(low)

        for half in range(2):
            by_rows(norm_out, half)
            send_part(early, u, half)

    def feed_backward(u):
        span = slice(u * unit, (u + 1) * unit)

        def back_out(block, some, across):
            own = pl.ds(u * unit + across.start, size)
            upstream = sends[(6 + u) * blocks + block, some, :].astype(f32)
            normal = stash[(5 + u) * blocks + block, some, :].astype(f32)
            add_sums(1, 1, upstream, normal)
            dz = whiten_back(upstream * gain(1, 1), normal, spreads[own, 1:2])
            dz_down[own, :] = dz.astype(low)

        for half in range(2):
            await_grad(u, half)
            by_rows(back_out, half)
        for c in range(4):
            d_hidden = dot_cols(dz_down[span, :], weight(8 + c))
            d_pre = (d_hidden * rhs[4 + c, span, :].astype(f32)).astype(low)
            rhs[4 + c, span, :] = d_pre
            add_branch(dot_cols(d_pre, weight(4 + c)), c == 0)

        def back_in(block, some, across):
            own = pl.ds(u * unit + across.start, size)
            normal, spread = whiten(kept[0, u, block, some, :].astype(f32))
            d_normed = total[2 * blocks + block, some, :]
            add_sums(1, 0, d_normed, normal)
            d_ln = whiten_back(d_normed * gain(1, 0), normal, spread)
            d_middle = (sends[(6 + u) * blocks + block, some, :].astype(f32) + d_ln).astype(low)
            kept[0, u, block, some, :] = d_middle
            upstream = d_middle.astype(f32)
            normal = stash[(2 + u) * blocks + block, some, :].astype(f32)
            add_sums(0, 1, upstream, normal)
            dz = whiten_back(upstream * gain(0, 1), normal, spreads[own, 0:1])
            stash[4 * blocks + block, some, :] = dz.astype(low)

        outputs_sent(u)
        by_rows(back_in)

    def attention_backward(u):
        span = slice(u * unit, (u + 1) * unit)
        keys = (u + 1) * unit
        lhs[1, :, span] = stash_read(4).T
        d_context = dot(stash_read(4), weight(3)).astype(low)
        stash_write(4, d_context)
        product = (d_context.astype(f32) * rhs[3, span, :].astype(f32)).astype(low)
        head = lax.broadcasted_iota(jnp.int32, (HEADS, width), 0)
        column = lax.broadcasted_iota(jnp.int32, (HEADS, width), 1)
        inside = (column >= head * HEAD) & (column < (head + 1) * HEAD)
        delta_t[...] = dot_cols(jnp.where(inside, 1.0, 0.0).astype(low), product)
        mask[:keys, :] = mask_of((keys, unit), 1, u * unit, 0)

        def pair(p, carry):
            lanes = pair_lanes(p)
            query = projected(0, lanes, u).astype(f32)
            key = projected(1, lanes, 0, u + 1)
            value = projected(2, lanes, 0, u + 1)
            d_out = stash[pl.ds(4 * blocks, blocks), :, lanes].reshape(unit, LANES).astype(f32)
            key_t = key.T
            d_key = d_value = None
            d_query = []
            for h in range(2):
                query_h = (query * half_lanes(h, score_scale)).astype(low)
                d_out_h = (d_out * half_lanes(h, 1.0)).astype(low)
                scores = dot_cols(key, query_h) + mask[:keys, :]
                prob = jnp.exp(scores - log_t[u, pl.ds(2 * p + h, 1), :])
                d_prob = dot_cols(value, d_out_h)
                d_scores = (prob * (d_prob - delta_t[pl.ds(2 * p + h, 1), :])).astype(low)
                term_v = dot(prob.astype(low), d_out_h)
                term_k = dot(d_scores, query_h)
                d_value = term_v if h == 0 else d_value + term_v
                d_key = term_k if h == 0 else d_key + term_k
                d_query.append(dot(key_t[h * HEAD : (h + 1) * HEAD, :], d_scores))
            d_query = jnp.concatenate(d_query, axis=0) * score_scale
            rhs[0, span, lanes] = d_query.T.astype(low)
            for i, grad in ((0, d_key), (1, d_value)):
                carried = pl.ds(i * blocks, blocks)
                if u == 1:
                    rhs[1 + i, span, lanes] = grad[unit:].astype(low)
                    total[carried, :, lanes] = grad[:unit].reshape(blocks, rows, LANES)
                else:
                    grad = grad + total[carried, :, lanes].reshape(unit, LANES)
                    rhs[1 + i, span, lanes] = grad.astype(low)
            return carry

        lax.fori_loop(0, PAIRS, pair, 0, unroll=2)
        for part in range(3):
            add_branch(dot_cols(rhs[part, span, :], weight(part)), part == 0)

        def back_in(block, some, across):
            normal, spread = whiten(stash[u * blocks + block, some, :].astype(f32))
            d_normed = total[2 * blocks + block, some, :]
            add_sums(0, 0, d_normed, normal)
            d_ln = whiten_back(d_normed * gain(0, 0), normal, spread)
            d_input = kept[0, u, block, some, :].astype(f32) + d_ln
            kept[1, u, block, some, :] = d_input.astype(low)

        for half in range(2):
            by_rows(back_in, half)
            send_part(late, 2 + u, half)

    def pair_block(step, stream=0):
        return jnp.where(step == 0, 6 * count, 6 * (step - 1)) + stream

    def ring_block(step, stream):
        return 12 * count - 6 * (step + 1) + stream

    def pair_slot(step):
        return jnp.where(lax.rem(step, 2) == 0, 5 * blocks, 0)

    def ring_slot(step):
        return jnp.where(lax.rem(step, 2) == 0, 6 * blocks, 0)

    def pair_copy(step):
        return to_peer(
            stash.at[pl.ds(pair_slot(step), 6)],
            pool.at[pl.ds(pair_block(step), 6)],
            pair_ss.at[lax.rem(step, 2)],
            pair_rs.at[step],
        )

    def pair_first(stream):
        return to_peer(
            stash.at[5 * blocks + stream],
            pool.at[6 * count + stream],
            first_ss.at[stream],
            first_rs.at[stream],
        )

    def ring_copy(step, stream):
        return pltpu.make_async_remote_copy(
            src_ref=sends.at[ring_slot(step) + stream],
            dst_ref=pool.at[ring_block(step, stream)],
            send_sem=ring_ss.at[lax.rem(step, 2), stream],
            recv_sem=ring_rs.at[step, stream],
            device_id=(jnp.where(stream < 3, right, left), section),
            device_id_type=MESH,
        )

    def ring_row(step, stream):
        behind = lax.rem(place + 2 * count - 1 - step, count)
        ahead = lax.rem(place + 1 + step, count)
        return ring_index(jnp.where(stream < 3, behind, ahead), count)

    def stream_of(group):
        return group + group // 2

    def product(step, group, part):
        block = ring_row(step, stream_of(group))
        side = jnp.where(part == 1, 2, jnp.where(group == 3, 1, 0))
        piece = lhs[side, pl.ds(pl.multiple_of(block * rows, rows), rows), :]
        return dot(piece, rhs[part * 4 + group])

    def down_product(step, turn, part):
        block = ring_row(step, 2 + 3 * turn)
        start = part * (2 * width) + block * (2 * rows) + turn * rows
        return dot(hidden_t[pl.ds(pl.multiple_of(start, rows), rows), :], dz_down[...])

    def each(count_of, action):
        def step(i, carry):
            action(i)
            return carry

        lax.fori_loop(0, count_of, step, 0)

    def pair_part(step):
        slot = pair_slot(step)

        def group_part(group):
            value = product(step, group, 1 - core)
            stash[slot + stream_of(group)] = value.astype(low)

        def down_part(turn):
            stash[slot + 2 + 3 * turn] = down_product(step, turn, 1 - core).astype(low)

        each(4, group_part)
        each(2, down_part)

    def own_part(step):
        def group_part(group):
            total[stream_of(group)] = product(step, group, core)

        def down_part(turn):
            total[2 + 3 * turn] = down_product(step, turn, core)

        each(4, group_part)
        each(2, down_part)

    def first_pair_group(group):
        stream = stream_of(group)
        stash[5 * blocks + stream] = product(0, group, 1 - core).astype(low)

    def first_pair_down(turn):
        stash[5 * blocks + 2 + 3 * turn] = down_product(0, turn, 1 - core).astype(low)

    def first_own_group(group):
        stream = stream_of(group)
        sends[6 * blocks + stream] = product(0, group, core).astype(low)

    def first_own_down(turn):
        sends[6 * blocks + 2 + 3 * turn] = down_product(0, turn, core).astype(low)

    def first_ring(stream):
        pair_first(stream).wait_recv()
        value = sends[6 * blocks + stream].astype(f32) + pool[6 * count + stream].astype(f32)
        sends[6 * blocks + stream] = value.astype(low)
        ring_copy(0, stream).start()

    def feed_first():
        for other in (left, right):
            pl.semaphore_signal(ready, inc=1, device_id=(other, section), device_id_type=MESH)
        pl.semaphore_signal(ready, inc=1, device_id=(dp, peer), device_id_type=MESH)
        each(2, first_pair_down)

        @pl.when(core == 0)
        def _():
            each(4, first_pair_group)

        pl.semaphore_wait(ready, 3)
        each(2, lambda turn: pair_first(2 + 3 * turn).start())

        @pl.when(core == 0)
        def _():
            each(4, lambda group: pair_first(stream_of(group)).start())

        each(2, first_own_down)

        @pl.when(core == 1)
        def _():
            each(4, first_own_group)

        each(2, lambda turn: first_ring(2 + 3 * turn))

        @pl.when(core == 1)
        def _():
            each(4, lambda group: first_ring(stream_of(group)))

    for u in range(2):
        attention_forward(u)
        feed_forward(u)
        for copy in out_copies(0, u):
            copy.start()

    feed_backward(1)
    attention_backward(1)
    for copy in out_copies(1, 1):
        copy.start()
    feed_backward(0)

    def last_attention(turn):
        pl.when(turn == jnp.where(early, 0, 1))(feed_first)

        @pl.when(turn == 0)
        def _():
            attention_backward(0)

    each(2, last_attention)
    for copy in out_copies(1, 0):
        copy.start()
    for k in range(8):
        (weight_remote(k) if k < 6 else affine_remote(k - 6)).wait_send()
    pl.semaphore_signal(pair_ready, inc=1, device_id=(dp, peer), device_id_type=MESH)

    @pl.when(core == 1)
    def _():
        each(4, first_pair_group)
        each(4, lambda group: pair_first(stream_of(group)).start())

    @pl.when(core == 0)
    def _():
        each(4, first_own_group)
        each(4, lambda group: first_ring(stream_of(group)))

    @pl.when(late)
    def _():
        for k in (2, 3):
            for half in range(2):
                hop_copy(k, half).wait_send()

    pair_part(1)
    pl.semaphore_wait(pair_ready, 1)
    pair_copy(1).start()
    own_part(1)

    slice_width = width // count
    for j in range(count):
        piece = sums[:, :, j * slice_width : (j + 1) * slice_width]
        small[j, :, :slice_width] = jnp.sum(piece, axis=1)

    gb_pair = to_peer(small, small_pair, small_sems.at[0], small_sems.at[1])

    def gb_copy(step):
        other = lax.rem(dp + step, count)
        return pltpu.make_async_remote_copy(
            src_ref=small_sum.at[other],
            dst_ref=small_recv.at[step],
            send_sem=small_ss.at[step],
            recv_sem=small_rs.at[step],
            device_id=(other, section),
            device_id_type=MESH,
        )

    gb_pair.start()
    gb_pair.wait()
    small_sum[...] = small[...] + small_pair[...]

    def gb_start(step, carry):
        gb_copy(step).start()
        return carry

    lax.fori_loop(1, count, gb_start, 0)

    for stream in range(6):
        pair_first(stream).wait_send()

    def ring_step(step, carry):
        pair_copy(step).wait_recv()

        def forward(i):
            turn = i // 2
            stream = 3 * lax.rem(i, 2) + jnp.where(turn == 0, 2, turn - 1)
            ring_copy(step - 1, stream).wait_recv()
            value = total[stream] + pool[pair_block(step, stream)].astype(f32)
            value = value + pool[ring_block(step - 1, stream)].astype(f32)

            @pl.when(step >= 2)
            def _():
                ring_copy(step - 2, stream).wait_send()

            sends[ring_slot(step) + stream] = value.astype(low)
            ring_copy(step, stream).start()

        each(6, forward)

        @pl.when(step >= 2)
        def _():
            pair_copy(step - 1).wait_send()

        pair_part(step + 1)
        pair_copy(step + 1).start()
        own_part(step + 1)
        return carry

    lax.fori_loop(1, count - 1, ring_step, 0)

    def grad_copy(stream):
        if stream % 3 < 2:
            group = stream % 3 + 2 * (stream // 3)
            target = first_grad.at[:, pl.ds(group * width, width)]
        else:
            target = down_grad.at[pl.ds((stream // 3) * rows, rows)]
        return pltpu.make_async_copy(total.at[stream], target, grad_ls.at[stream])

    last = count - 1
    pair_copy(last).wait_recv()
    for stream in (2, 5, 0, 3, 1, 4):
        total[stream] += pool[pair_block(last, stream)].astype(f32)
        ring_copy(last - 1, stream).wait_recv()
        total[stream] += pool[ring_block(last - 1, stream)].astype(f32)
        grad_copy(stream).start()

    small_out[...] = small_sum[dp]

    def gb_finish(step, carry):
        gb_copy(step).wait()
        small_out[...] += small_recv[step]
        return carry

    lax.fori_loop(1, count, gb_finish, 0)
    for stream in range(6):
        ring_copy(last - 1, stream).wait_send()
        ring_copy(last - 2, stream).wait_send()
        grad_copy(stream).wait()
    pair_copy(last).wait_send()
    pair_copy(last - 1).wait_send()
    for u in range(2):
        out_copies(0, u)[1].wait_recv()
        local_copy, remote_copy = out_copies(1, u)
        local_copy.wait()
        remote_copy.wait()


def layers(tokens, cotangent, lengths, first, down, gains, biases):
    count = lax.axis_size("dp")
    token_count, width = tokens.shape
    row_len = token_count // lengths.shape[0]
    unit = row_len // 2
    rows = width // count
    blocks = unit // rows
    vmem = pl.BlockSpec(memory_space=pltpu.VMEM)
    anywhere = pl.BlockSpec(memory_space=pl.ANY)
    sem = pltpu.SemaphoreType.DMA
    shape = jax.ShapeDtypeStruct
    buffer = pltpu.VMEM
    cut = (token_count // rows, rows, width)
    small = (count, 8, max(128, width // count))
    outs = pl.pallas_call(
        functools.partial(layers_kernel, count),
        out_shape=(
            shape(cut, low),
            shape(cut, low),
            shape((rows, 4 * width), f32),
            shape((2 * rows, width), f32),
            shape(small[1:], f32),
        ),
        in_specs=[anywhere, anywhere, pl.BlockSpec(memory_space=pltpu.SMEM)] + [anywhere] * 4,
        out_specs=(anywhere, anywhere, anywhere, anywhere, vmem),
        scratch_shapes=[
            buffer((12 * count, rows, width), low),
            buffer((8 * blocks + max(0, 6 - 2 * blocks), rows, width), low),
            buffer((7 * blocks + max(0, 6 - 2 * blocks), rows, width), low),
            buffer((row_len, 128), f32),
            buffer((2, 2, blocks, rows, width), low),
            buffer((row_len, unit), f32),
            buffer((max(6, 3 * blocks), rows, width), f32),
            buffer((3, width, row_len), low),
            buffer((4 * width, row_len), low),
            buffer((8, row_len, width), low),
            buffer((row_len, width), low),
            buffer((2, 2, 2, width), f32),
            buffer((2, HEADS, unit), f32),
            buffer((unit, LANES), f32),
            buffer((HEADS, unit), f32),
            buffer((8, 8, width), f32),
            buffer(small, f32),
            buffer(small, f32),
            buffer(small, f32),
            buffer(small, f32),
            sem((8,)),
            sem((8,)),
            sem((8,)),
            sem((4,)),
            sem((4, 2)),
            sem((4, 2)),
            sem((4,)),
            sem((4,)),
            sem((4,)),
            pltpu.SemaphoreType.REGULAR,
            pltpu.SemaphoreType.REGULAR,
            sem((6,)),
            sem((6,)),
            sem((2,)),
            sem((count,)),
            sem((2, 6)),
            sem((count - 1, 6)),
            sem((2,)),
            sem((count,)),
            sem((count,)),
            sem((6,)),
        ],
        compiler_params=pltpu.CompilerParams(
            collective_id=0, has_side_effects=True, vmem_limit_bytes=63 * 1024 * 1024
        ),
        name="layers",
    )(
        tokens.reshape(cut),
        cotangent.reshape(cut),
        lengths,
        first.reshape(count, rows, 4 * width),
        down.reshape(2 * count, rows, width),
        gains,
        biases,
    )
    return outs


def place_kernel(*refs):
    sources, small, targets, (gain_grad, bias_grad) = refs[:4], refs[4], refs[5:9], refs[9:11]
    buffers, (arrived, written) = refs[11:15], refs[15:]
    reads, writes = [], []
    for j in range(4):
        for i, (source, target, buffer) in enumerate(zip(sources, targets, buffers)):
            size = max(16, source.shape[0] // 4)
            if j * size >= source.shape[0]:
                continue
            some = pl.ds(j * size, size)
            reads.append(
                pltpu.make_async_copy(source.at[some], buffer.at[some], arrived.at[i, j])
            )
            writes.append(
                pltpu.make_async_copy(buffer.at[some], target.at[0, some], written.at[i, j])
            )
    for read in reads:
        read.start()
    feed = lax.axis_index("section") % 2 == 1
    width = gain_grad.shape[2]
    gain_grad[0] = jnp.where(feed, small[4:6, :width], small[0:2, :width])
    bias_grad[0] = jnp.where(feed, small[6:8, :width], small[2:4, :width])
    for read, write in zip(reads, writes):
        read.wait()
        write.start()
    for write in writes:
        write.wait()


def local(tokens, doc_lengths, first_weights, down_weights, norm_gains, norm_biases, cotangent):
    width = tokens.shape[1]
    outputs, input_grads, first_part, down_part, small = layers(
        tokens,
        cotangent,
        doc_lengths,
        first_weights[0],
        down_weights[0],
        norm_gains,
        norm_biases,
    )
    slice_width = width // lax.axis_size("dp")
    results = [outputs.reshape(tokens.shape), input_grads.reshape(tokens.shape)]
    results += [first_part, down_part]
    norm_part = jax.ShapeDtypeStruct((1, 2, slice_width), f32)
    anywhere = pl.BlockSpec(memory_space=pl.ANY)
    vmem = pl.BlockSpec(memory_space=pltpu.VMEM)
    return pl.pallas_call(
        place_kernel,
        out_shape=[jax.ShapeDtypeStruct((1,) + r.shape, r.dtype) for r in results]
        + [norm_part, norm_part],
        in_specs=[anywhere] * 4 + [vmem],
        out_specs=[anywhere] * 4 + [vmem] * 2,
        scratch_shapes=[pltpu.VMEM(r.shape, r.dtype) for r in results]
        + [pltpu.SemaphoreType.DMA((4, 4))] * 2,
        name="place",
    )(*results, small)


def solution(mesh):
    placed = (
        P("dp", None),
        P("dp", None),
        P("section", None, None),
        P("section", None, None),
        P("section", None, None),
        P("section", None, None),
        P("dp", None),
    )
    return jax.shard_map(
        local,
        mesh=mesh,
        in_specs=placed,
        out_specs=(
            P("section", "dp", None),
            P("section", "dp", None),
            P("section", "dp", None),
            P("section", "dp", None),
            P("section", None, "dp"),
            P("section", None, "dp"),
        ),
        check_vma=False,
    )
```

profile of v0, /device:TPU:0, one launch (start us, length us, event | category | flops | bytes accessed | tf_op | source)
XLA Modules:
  0.0 258.8 jit_solution(13143555292700346877)
XLA Ops:
  0.6 250.8 %layers.1 = (bf16[8,128,1024]{2,1,0:T(8,128)(2,1)}, bf16[8,128,1024]{2,1,0:T(8,128)(2,1)}, f32[128,4096]{1,0:T(8,128)}, f32[256,1024]{1,0:T(8,128)}, f32[8,128]{1,0:T(8,128)}) custom-call(bf16[8,128,1024]{2,1,0:T(8,128)(2,1)} %bitcast.8, bf16[8,128,1024]{2,1,0:T(8,128)(2,1)} %bitcast.9, s32[2,4]{1,0:T(2,128)} %lengths.1, bf16[8,128,4096]{2,1,0:T(8,128)(2,1)} %bitcast.6, ...), custom_call_target="tpu_custom_call" | custom-call | tf_op jit(solution)/shard_map/layers/pallas_call | solution.py:862
  251.4 7.2 %place.1 = (bf16[1,1024,1024]{2,1,0:T(8,128)(2,1)}, bf16[1,1024,1024]{2,1,0:T(8,128)(2,1)}, f32[1,128,4096]{2,1,0:T(8,128)}, f32[1,256,1024]{2,1,0:T(8,128)}, f3...) custom-call(bf16[1024,1024]{1,0:T(8,128)(2,1)} %bitcast.10, bf16[1024,1024]{1,0:T(8,128)(2,1)} %bitcast.11, ...), custom_call_target="tpu_custom_call" | custom-call | tf_op jit(solution)/shard_map/place/pallas_call | solution.py:978
where the time goes:
time: 262 us; the launch traced here: 259 us
  Pallas kernels  258 us (98%)
    pallas_call x1, Pallas kernels, layers(): pl.pallas_call(functools.partial(layers_kernel, count), out_shape=(shape(...  251 us
    pallas_call x1, Pallas kernels, local(): pl.pallas_call(place_kernel, out_shape=[jax.ShapeDtypeStruct((1,) + r.sha...  7.21 us

commit v1 on v0

--- a/solution.py
+++ b/solution.py
@@ -383,24 +383,46 @@
             values = stash[u * blocks + block, some, :].astype(f32)
             stash[4 * blocks + block, some, :] = normed_input(0, values)
 
-        for half in range(2):
-            await_input(u, half)
-            by_rows(norm_in, half)
-            if u == 0:
-                part_blocks = blocks // 2
-                normed = stash[pl.ds(4 * blocks + half * part_blocks, part_blocks)]
-                for part in range(3):
-                    if half == 0:
-                        await_chunk(part)
-                    value = dot(normed.reshape(unit // 2, width), weight(part)).astype(low)
-                    target = pl.ds(2 * part * blocks + half * part_blocks, part_blocks)
-                    sends[target] = value.reshape(part_blocks, rows, width)
-        for part in range(3) if u == 1 else ():
-            value = dot(stash_read(4), weight(part)).astype(low)
-            sends[pl.ds((2 * part + u) * blocks, blocks)] = value.reshape(blocks, rows, width)
-        lhs[0, :, span] = stash_read(4).T
         for i in range(u + 1):
             mask[i * unit : (i + 1) * unit, :] = mask_of((unit, unit), 0, u * unit, i * unit)
+
+        def project_all(stage_weights):
+            for part in range(3):
+                if stage_weights:
+                    await_chunk(part)
+                value = dot(stash_read(4), weight(part)).astype(low)
+                target = pl.ds((2 * part + u) * blocks, blocks)
+                sends[target] = value.reshape(blocks, rows, width)
+
+        if u == 1:
+            for half in range(2):
+                await_input(u, half)
+                by_rows(norm_in, half)
+            project_all(False)
+        else:
+
+            @pl.when(early)
+            def _():
+                token_copy(u).wait()
+                by_rows(norm_in)
+                project_all(True)
+
+            @pl.when(late)
+            def _():
+                for part in range(3):
+                    await_chunk(part)
+                part_blocks = blocks // 2
+                for half in range(2):
+                    hop_copy(u, half).wait_recv()
+                    by_rows(norm_in, half)
+                    normed = stash[pl.ds(4 * blocks + half * part_blocks, part_blocks)]
+                    normed = normed.reshape(unit // 2, width)
+                    for part in range(3):
+                        value = dot(normed, weight(part)).astype(low)
+                        target = pl.ds(2 * part * blocks + half * part_blocks, part_blocks)
+                        sends[target] = value.reshape(part_blocks, rows, width)
+
+        lhs[0, :, span] = stash_read(4).T
         lane = lax.broadcasted_iota(jnp.int32, (unit, LANES), 1)
 
         def pair(p, carry):
@@ -409,21 +431,21 @@
             key = projected(1, lanes, 0, u + 1)
             value = projected(2, lanes, 0, u + 1)
             added = jnp.concatenate([mask[i * unit : (i + 1) * unit, :] for i in range(u + 1)], 1)
-            context = None
-            for h in range(2):
-                scores = dot_cols((query * half_lanes(h, score_scale)).astype(low), key)
-                scores = scores + added
-                top = jnp.max(scores, axis=-1, keepdims=True)
-                exponent = jnp.exp(scores - top)
-                summed = jnp.sum(exponent, axis=-1, keepdims=True)
-                part = dot(exponent.astype(low), value) * (1.0 / summed)
-                context = part if h == 0 else jnp.where(lane < HEAD, context, part)
-                log_total = top + jnp.log(summed)
-                log_rows[...] = jnp.where(lane == 2 * p + h, log_total, log_rows[...])
+            both = [(query * half_lanes(h, score_scale)).astype(low) for h in range(2)]
+            scores = dot_cols(jnp.concatenate(both, axis=0), key)
+            scores = scores + jnp.concatenate([added, added], axis=0)
+            top = jnp.max(scores, axis=-1, keepdims=True)
+            exponent = jnp.exp(scores - top)
+            summed = jnp.sum(exponent, axis=-1, keepdims=True)
+            context = dot(exponent.astype(low), value) * (1.0 / summed)
+            log_total = top + jnp.log(summed)
+            logs = jnp.where(lane == 2 * p, log_total[:unit], log_rows[...])
+            log_rows[...] = jnp.where(lane == 2 * p + 1, log_total[unit:], logs)
+            context = jnp.where(lane < HEAD, context[:unit], context[unit:])
             rhs[3, span, lanes] = context.astype(low)
             return carry
 
-        lax.fori_loop(0, PAIRS, pair, 0, unroll=2)
+        lax.fori_loop(0, PAIRS, pair, 0, unroll=4)
         log_t[u] = log_rows[...].T[:HEADS]
         if u == 0:
             await_chunk(3)
@@ -500,6 +522,12 @@
             stash[4 * blocks + block, some, :] = dz.astype(low)
 
         outputs_sent(u)
+        if u == 0:
+            for other in (left, right):
+                pl.semaphore_signal(
+                    ready, inc=1, device_id=(other, section), device_id_type=MESH
+                )
+            pl.semaphore_signal(ready, inc=1, device_id=(dp, peer), device_id_type=MESH)
         by_rows(back_in)
 
     def attention_backward(u):
@@ -522,20 +550,24 @@
             value = projected(2, lanes, 0, u + 1)
             d_out = stash[pl.ds(4 * blocks, blocks), :, lanes].reshape(unit, LANES).astype(f32)
             key_t = key.T
-            d_key = d_value = None
-            d_query = []
-            for h in range(2):
-                query_h = (query * half_lanes(h, score_scale)).astype(low)
-                d_out_h = (d_out * half_lanes(h, 1.0)).astype(low)
-                scores = dot_cols(key, query_h) + mask[:keys, :]
-                prob = jnp.exp(scores - log_t[u, pl.ds(2 * p + h, 1), :])
-                d_prob = dot_cols(value, d_out_h)
-                d_scores = (prob * (d_prob - delta_t[pl.ds(2 * p + h, 1), :])).astype(low)
-                term_v = dot(prob.astype(low), d_out_h)
-                term_k = dot(d_scores, query_h)
-                d_value = term_v if h == 0 else d_value + term_v
-                d_key = term_k if h == 0 else d_key + term_k
-                d_query.append(dot(key_t[h * HEAD : (h + 1) * HEAD, :], d_scores))
+            heads = range(2)
+            query_both = [(query * half_lanes(h, score_scale)).astype(low) for h in heads]
+            query_both = jnp.concatenate(query_both, axis=0)
+            d_out_both = [(d_out * half_lanes(h, 1.0)).astype(low) for h in heads]
+            d_out_both = jnp.concatenate(d_out_both, axis=0)
+            logs = jnp.concatenate([log_t[u, pl.ds(2 * p + h, 1), :] for h in heads], axis=1)
+            delta = jnp.concatenate([delta_t[pl.ds(2 * p + h, 1), :] for h in heads], axis=1)
+            added = mask[:keys, :]
+            scores = dot_cols(key, query_both) + jnp.concatenate([added, added], axis=1)
+            prob = jnp.exp(scores - logs)
+            d_prob = dot_cols(value, d_out_both)
+            d_scores = (prob * (d_prob - delta)).astype(low)
+            d_value = dot(prob.astype(low), d_out_both)
+            d_key = dot(d_scores, query_both)
+            d_query = [
+                dot(key_t[h * HEAD : (h + 1) * HEAD, :], d_scores[:, h * unit : (h + 1) * unit])
+                for h in heads
+            ]
             d_query = jnp.concatenate(d_query, axis=0) * score_scale
             rhs[0, span, lanes] = d_query.T.astype(low)
             for i, grad in ((0, d_key), (1, d_value)):
@@ -548,7 +580,7 @@
                     rhs[1 + i, span, lanes] = grad.astype(low)
             return carry
 
-        lax.fori_loop(0, PAIRS, pair, 0, unroll=2)
+        lax.fori_loop(0, PAIRS, pair, 0, unroll=4)
         for part in range(3):
             add_branch(dot_cols(rhs[part, span, :], weight(part)), part == 0)
 
@@ -651,9 +683,14 @@
         each(4, group_part)
         each(2, down_part)
 
-    def first_pair_group(group):
+    def turn_about(i):
+        return i // 2 + 2 * lax.rem(i, 2)
+
+    def first_pair_group(i):
+        group = turn_about(i)
         stream = stream_of(group)
         stash[5 * blocks + stream] = product(0, group, 1 - core).astype(low)
+        pair_first(stream).start()
 
     def first_pair_down(turn):
         stash[5 * blocks + 2 + 3 * turn] = down_product(0, turn, 1 - core).astype(low)
@@ -664,6 +701,9 @@
 
     def first_own_down(turn):
         sends[6 * blocks + 2 + 3 * turn] = down_product(0, turn, core).astype(low)
+
+    def first_ring_group(i):
+        first_ring(stream_of(turn_about(i)))
 
     def first_ring(stream):
         pair_first(stream).wait_recv()
@@ -672,23 +712,14 @@
         ring_copy(0, stream).start()
 
     def feed_first():
-        for other in (left, right):
-            pl.semaphore_signal(ready, inc=1, device_id=(other, section), device_id_type=MESH)
-        pl.semaphore_signal(ready, inc=1, device_id=(dp, peer), device_id_type=MESH)
         each(2, first_pair_down)
-
-        @pl.when(core == 0)
-        def _():
-            each(4, first_pair_group)
-
         pl.semaphore_wait(ready, 3)
         each(2, lambda turn: pair_first(2 + 3 * turn).start())
+        each(2, first_own_down)
 
         @pl.when(core == 0)
         def _():
-            each(4, lambda group: pair_first(stream_of(group)).start())
-
-        each(2, first_own_down)
+            each(4, first_pair_group)
 
         @pl.when(core == 1)
         def _():
@@ -698,7 +729,7 @@
 
         @pl.when(core == 1)
         def _():
-            each(4, lambda group: first_ring(stream_of(group)))
+            each(4, first_ring_group)
 
     for u in range(2):
         attention_forward(u)
@@ -729,12 +760,11 @@
     @pl.when(core == 1)
     def _():
         each(4, first_pair_group)
-        each(4, lambda group: pair_first(stream_of(group)).start())
 
     @pl.when(core == 0)
     def _():
         each(4, first_own_group)
-        each(4, lambda group: first_ring(stream_of(group)))
+        each(4, first_ring_group)
 
     @pl.when(late)
     def _():
@@ -933,18 +963,9 @@
     sources, small, targets, (gain_grad, bias_grad) = refs[:4], refs[4], refs[5:9], refs[9:11]
     buffers, (arrived, written) = refs[11:15], refs[15:]
     reads, writes = [], []
-    for j in range(4):
-        for i, (source, target, buffer) in enumerate(zip(sources, targets, buffers)):
-            size = max(16, source.shape[0] // 4)
-            if j * size >= source.shape[0]:
-                continue
-            some = pl.ds(j * size, size)
-            reads.append(
-                pltpu.make_async_copy(source.at[some], buffer.at[some], arrived.at[i, j])
-            )
-            writes.append(
-                pltpu.make_async_copy(buffer.at[some], target.at[0, some], written.at[i, j])
-            )
+    for i, (source, target, buffer) in enumerate(zip(sources, targets, buffers)):
+        reads.append(pltpu.make_async_copy(source, buffer, arrived.at[i]))
+        writes.append(pltpu.make_async_copy(buffer, target.at[0], written.at[i]))
     for read in reads:
         read.start()
     feed = lax.axis_index("section") % 2 == 1
@@ -982,7 +1003,7 @@
         in_specs=[anywhere] * 4 + [vmem],
         out_specs=[anywhere] * 4 + [vmem] * 2,
         scratch_shapes=[pltpu.VMEM(r.shape, r.dtype) for r in results]
-        + [pltpu.SemaphoreType.DMA((4, 4))] * 2,
+        + [pltpu.SemaphoreType.DMA((4,))] * 2,
         name="place",
     )(*results, small)
 

time: 262 us -> 257 us (0.981)
  Pallas kernels: 258 us -> 252 us
    pallas_call x1, Pallas kernels: 251 us -> 245 us  [layers(): pl.pallas_call(functools.partial(layers_kernel, count), out_shape=(shape(...]
where the time goes in v1:
time: 257 us; the launch traced here: 253 us
  Pallas kernels  252 us (98%)
    pallas_call x1, Pallas kernels, layers(): pl.pallas_call(functools.partial(layers_kernel, count), out_shape=(shape(...  245 us
    pallas_call x1, Pallas kernels, local(): pl.pallas_call(place_kernel, out_shape=[jax.ShapeDtypeStruct((1,) + r.sha...  6.77 us

profile of v1, /device:TPU:0, one launch (start us, length us, event | category | flops | bytes accessed | tf_op | source)
XLA Modules:
  0.0 253.2 jit_solution(275095160952676800)
XLA Ops:
  0.6 245.3 %layers.1 = (bf16[8,128,1024]{2,1,0:T(8,128)(2,1)}, bf16[8,128,1024]{2,1,0:T(8,128)(2,1)}, f32[128,4096]{1,0:T(8,128)}, f32[256,1024]{1,0:T(8,128)}, f32[8,128]{1,0:T(8,128)}) custom-call(bf16[8,128,1024]{2,1,0:T(8,128)(2,1)} %bitcast.8, bf16[8,128,1024]{2,1,0:T(8,128)(2,1)} %bitcast.9, s32[2,4]{1,0:T(2,128)} %lengths.1, bf16[8,128,4096]{2,1,0:T(8,128)(2,1)} %bitcast.6, ...), custom_call_target="tpu_custom_call" | custom-call | tf_op jit(solution)/shard_map/layers/pallas_call | solution.py:892
  246.0 6.8 %place.1 = (bf16[1,1024,1024]{2,1,0:T(8,128)(2,1)}, bf16[1,1024,1024]{2,1,0:T(8,128)(2,1)}, f32[1,128,4096]{2,1,0:T(8,128)}, f32[1,256,1024]{2,1,0:T(8,128)}, f3...) custom-call(bf16[1024,1024]{1,0:T(8,128)(2,1)} %bitcast.10, bf16[1024,1024]{1,0:T(8,128)(2,1)} %bitcast.11, ...), custom_call_target="tpu_custom_call" | custom-call | tf_op jit(solution)/shard_map/place/pallas_call | solution.py:999

commit v2 on v1

--- a/solution.py
+++ b/solution.py
@@ -196,6 +196,7 @@
         def _():
             weight_local((i + 2) % 4).wait()
 
+    def await_down(i):
         if i < 2:
             weight_local(4 + i).wait()
         else:
@@ -465,16 +466,6 @@
     def feed_forward(u):
         span = slice(u * unit, (u + 1) * unit)
         lhs[2, :, span] = stash_read(4).T
-        for i in range(4):
-            c = lax.rem(2 * core + i, 4) if u == 0 else i
-            if u == 0:
-                await_feed(i)
-            hidden, slope = gelu_both(dot(stash_read(4), weight(4 + c)))
-            hidden = hidden.astype(low)
-            rhs[4 + c, span, :] = slope.astype(low)
-            hidden_t[pl.ds(pl.multiple_of(c * width, width), width), span] = hidden.T
-            add_branch(dot(hidden, weight(8 + c)), i == 0)
-
         def norm_out(block, some, across):
             normal, spread = whiten(total[2 * blocks + block, some, :])
             stash[(5 + u) * blocks + block, some, :] = normal.astype(low)
@@ -483,9 +474,44 @@
             output = middle + (normal * gain(1, 1) + bias(1, 1))
             kept[1, u, block, some, :] = output.astype(low)
 
-        for half in range(2):
-            by_rows(norm_out, half)
-            send_part(early, u, half)
+        def whole():
+            for i in range(4):
+                c = lax.rem(2 * core + i, 4) if u == 0 else i
+                if u == 0:
+                    await_feed(i)
+                hidden, slope = gelu_both(dot(stash_read(4), weight(4 + c)))
+                hidden = hidden.astype(low)
+                rhs[4 + c, span, :] = slope.astype(low)
+                hidden_t[pl.ds(pl.multiple_of(c * width, width), width), span] = hidden.T
+                if u == 0:
+                    await_down(i)
+                add_branch(dot(hidden, weight(8 + c)), i == 0)
+            for half in range(2):
+                by_rows(norm_out, half)
+                send_part(early, u, half)
+
+        def by_halves():
+            part_blocks, part_rows = blocks // 2, unit // 2
+            for half in range(2):
+                some = slice(u * unit + half * part_rows, u * unit + (half + 1) * part_rows)
+                sum_at = pl.ds(2 * blocks + half * part_blocks, part_blocks)
+                normed = stash[pl.ds(4 * blocks + half * part_blocks, part_blocks)]
+                normed = normed.reshape(part_rows, width)
+                for c in range(4):
+                    hidden, slope = gelu_both(dot(normed, weight(4 + c)))
+                    hidden = hidden.astype(low)
+                    rhs[4 + c, some, :] = slope.astype(low)
+                    hidden_t[c * width : (c + 1) * width, some] = hidden.T
+                    term = dot(hidden, weight(8 + c)).reshape(part_blocks, rows, width)
+                    total[sum_at] = term if c == 0 else total[sum_at] + term
+                by_rows(norm_out, half)
+                hop_copy(u, half).start()
+
+        if u == 0:
+            whole()
+        else:
+            pl.when(early)(by_halves)
+            pl.when(late)(whole)
 
     def feed_backward(u):
         span = slice(u * unit, (u + 1) * unit)

time: 257 us -> 253 us (0.984)
  Pallas kernels: 252 us -> 249 us
    pallas_call x1, Pallas kernels: 245 us -> 242 us  [layers(): pl.pallas_call(functools.partial(layers_kernel, count), out_shape=(shape(...]
where the time goes in v2:
time: 253 us; the launch traced here: 250 us
  Pallas kernels  249 us (98%)
    pallas_call x1, Pallas kernels, layers(): pl.pallas_call(functools.partial(layers_kernel, count), out_shape=(shape(...  242 us
    pallas_call x1, Pallas kernels, local(): pl.pallas_call(place_kernel, out_shape=[jax.ShapeDtypeStruct((1,) + r.sha...  6.77 us

profile of v2, /device:TPU:0, one launch (start us, length us, event | category | flops | bytes accessed | tf_op | source)
XLA Modules:
  0.0 249.9 jit_solution(2962756070152305926)
XLA Ops:
  0.6 242.3 %layers.1 = (bf16[8,128,1024]{2,1,0:T(8,128)(2,1)}, bf16[8,128,1024]{2,1,0:T(8,128)(2,1)}, f32[128,4096]{1,0:T(8,128)}, f32[256,1024]{1,0:T(8,128)}, f32[8,128]{1,0:T(8,128)}) custom-call(bf16[8,128,1024]{2,1,0:T(8,128)(2,1)} %bitcast.8, bf16[8,128,1024]{2,1,0:T(8,128)(2,1)} %bitcast.9, s32[2,4]{1,0:T(2,128)} %lengths.1, bf16[8,128,4096]{2,1,0:T(8,128)(2,1)} %bitcast.6, ...), custom_call_target="tpu_custom_call" | custom-call | tf_op jit(solution)/shard_map/layers/pallas_call | solution.py:918
  242.9 6.8 %place.1 = (bf16[1,1024,1024]{2,1,0:T(8,128)(2,1)}, bf16[1,1024,1024]{2,1,0:T(8,128)(2,1)}, f32[1,128,4096]{2,1,0:T(8,128)}, f32[1,256,1024]{2,1,0:T(8,128)}, f3...) custom-call(bf16[1024,1024]{1,0:T(8,128)(2,1)} %bitcast.10, bf16[1024,1024]{1,0:T(8,128)(2,1)} %bitcast.11, ...), custom_call_target="tpu_custom_call" | custom-call | tf_op jit(solution)/shard_map/place/pallas_call | solution.py:1025

commit v3 on v2

--- a/solution.py
+++ b/solution.py
@@ -554,6 +554,7 @@
                     ready, inc=1, device_id=(other, section), device_id_type=MESH
                 )
             pl.semaphore_signal(ready, inc=1, device_id=(dp, peer), device_id_type=MESH)
+            pl.when(early)(down_first)
         by_rows(back_in)
 
     def attention_backward(u):
@@ -737,11 +738,15 @@
         sends[6 * blocks + stream] = value.astype(low)
         ring_copy(0, stream).start()
 
-    def feed_first():
+    def down_first():
         each(2, first_pair_down)
+        each(2, first_own_down)
         pl.semaphore_wait(ready, 3)
         each(2, lambda turn: pair_first(2 + 3 * turn).start())
-        each(2, first_own_down)
+
+    def feed_first():
+        pl.when(late)(down_first)
+        each(2, lambda turn: first_ring(2 + 3 * turn))
 
         @pl.when(core == 0)
         def _():
@@ -750,11 +755,6 @@
         @pl.when(core == 1)
         def _():
             each(4, first_own_group)
-
-        each(2, lambda turn: first_ring(2 + 3 * turn))
-
-        @pl.when(core == 1)
-        def _():
             each(4, first_ring_group)
 
     for u in range(2):

time: 253 us -> 254 us (level)
  no operation moved by 1% of the time
where the time goes in v3:
time: 254 us; the launch traced here: 250 us
  Pallas kernels  249 us (98%)
    pallas_call x1, Pallas kernels, layers(): pl.pallas_call(functools.partial(layers_kernel, count), out_shape=(shape(...  243 us
    pallas_call x1, Pallas kernels, local(): pl.pallas_call(place_kernel, out_shape=[jax.ShapeDtypeStruct((1,) + r.sha...  6.77 us

profile of v3, /device:TPU:0, one launch (start us, length us, event | category | flops | bytes accessed | tf_op | source)
XLA Modules:
  0.0 250.2 jit_solution(2793759725542425168)
XLA Ops:
  0.6 242.6 %layers.1 = (bf16[8,128,1024]{2,1,0:T(8,128)(2,1)}, bf16[8,128,1024]{2,1,0:T(8,128)(2,1)}, f32[128,4096]{1,0:T(8,128)}, f32[256,1024]{1,0:T(8,128)}, f32[8,128]{1,0:T(8,128)}) custom-call(bf16[8,128,1024]{2,1,0:T(8,128)(2,1)} %bitcast.8, bf16[8,128,1024]{2,1,0:T(8,128)(2,1)} %bitcast.9, s32[2,4]{1,0:T(2,128)} %lengths.1, bf16[8,128,4096]{2,1,0:T(8,128)(2,1)} %bitcast.6, ...), custom_call_target="tpu_custom_call" | custom-call | tf_op jit(solution)/shard_map/layers/pallas_call | solution.py:918
  243.2 6.8 %place.1 = (bf16[1,1024,1024]{2,1,0:T(8,128)(2,1)}, bf16[1,1024,1024]{2,1,0:T(8,128)(2,1)}, f32[1,128,4096]{2,1,0:T(8,128)}, f32[1,256,1024]{2,1,0:T(8,128)}, f3...) custom-call(bf16[1024,1024]{1,0:T(8,128)(2,1)} %bitcast.10, bf16[1024,1024]{1,0:T(8,128)(2,1)} %bitcast.11, ...), custom_call_target="tpu_custom_call" | custom-call | tf_op jit(solution)/shard_map/place/pallas_call | solution.py:1025
